TPU v7x, 32 devices: a whole 2x2x4 slice. The times are simulated.
32 devices in a mesh: rep: 8 (over y, x, core), shard: 4 (over z).
Axes of the slice: x: 2, y: 2, z: 4, core: 2. Of those that a mesh axis runs over, the one named last changes fastest.
Arguments:
- gradients: bfloat16 [8, 96, 2560], P(None, 'shard')
- momentum: float32 [8, 96, 2560], P(None, 'shard'), may hold values from -60 to 60
Outputs:
- updates: bfloat16 [8, 96, 2560], P(None, 'shard', 'rep')
- new_momentum: float32 [8, 96, 2560], P(None, 'shard')
All inputs are finite; a program needn't handle non-finite values.
Results may differ from a plain program's by a relative error of at most 0.0014.
Values may be sent and summed in bfloat16 or wider, within the bound.
A program may use at most 64 MiB of HBM per device.

v0:
```python
import math
import jax
import jax.numpy as jnp
from jax import lax
from jax.sharding import PartitionSpec as P

ITERS = 5
momentum_decay = 0.95
norm_floor = 1e-07
quintic_terms = (3.4445, -4.775, 2.0315)


def mm(a, b):
    return jnp.einsum("kij,kjl->kil", a, b, precision=lax.Precision.HIGHEST)


def schulz_factor(gram, scale):
    total = jnp.trace(gram, axis1=1, axis2=2)[:, None, None]
    inverse = 1.0 / (jnp.sqrt(total) + norm_floor)
    g = jnp.where(inverse > 0, gram * inverse * inverse, 0.0)
    eye = jnp.eye(gram.shape[-1], dtype=jnp.float32)
    a, b, c = quintic_terms
    q = None
    for turn in range(ITERS):
        poly = a * eye + b * g + c * mm(g, g)
        q = poly if q is None else mm(poly, q)
        if turn < ITERS - 1:
            g = mm(poly, mm(poly, g))
    return q * (scale * inverse)


def per_device_plain(gradients, momentum):
    rows, width = gradients.shape[1:]
    scale = 0.2 * math.sqrt(max(rows * lax.axis_size("shard"), width))
    replicas = lax.axis_size("rep")
    grads = gradients.astype(jnp.float32)
    new_momentum = momentum_decay * momentum + grads
    effective = grads + momentum_decay * new_momentum
    cols = width // replicas
    mine = lax.dynamic_slice_in_dim(effective, lax.axis_index("rep") * cols, cols, 2)
    whole = lax.all_to_all(mine, "shard", split_axis=0, concat_axis=1, tiled=True)
    gram = jnp.einsum("kij,klj->kil", whole, whole, precision=lax.Precision.HIGHEST)
    factor = schulz_factor(lax.psum(gram, "rep"), scale)
    out = mm(factor, whole).astype(jnp.bfloat16)
    return (lax.all_to_all(out, "shard", split_axis=1, concat_axis=0, tiled=True), new_momentum)


def solution(mesh):
    in_specs = (P(None, "shard", None), P(None, "shard", None))
    out_specs = (P(None, "shard", "rep"), P(None, "shard", None))
    return jax.shard_map(
        per_device_plain, mesh=mesh, in_specs=in_specs, out_specs=out_specs, check_vma=False
    )
```

profile of v0, /device:TPU:0, one launch (start us, length us, event | category | flops | bytes accessed | tf_op | source)
XLA Modules:
  0.0 107.0 jit_solution(3335476174348482193)
XLA Ops:
  7.2 0.0 copy-start
  7.2 0.0 copy-start.2
  7.2 2.9 %convert_element_type.7 = f32[8,24,2560]{2,1,0:T(8,128)} convert(bf16[8,24,2560]{2,1,0:T(8,128)(2,1)} %param.2) | non-fusion elementwise | flops 491520 | bytes 2949120 | tf_op jit(solution)/shard_map/convert_element_type | solution.py:36
  10.1 0.0 copy-done
  10.1 0.0 copy-done.2
  10.1 0.3 multiply_add_fusion
  10.3 0.0 copy-start.1
  10.3 2.2 %dynamic-slice_add_fusion = f32[8,24,320]{2,1,0:T(8,128)} fusion(f32[8,24,2560]{2,1,0:T(8,128)} %convert_element_type.7, s32[]{:T(128)S(6)} %select_n.12, f32[8,24,2560]{2,1,0:T(8,128)S(1)} %multiply_add_fusion), kind=kLoop, calls=%fused_computation.13 | loop fusion | flops 122880 | bytes 737284 | tf_op jit(solution)/shard_map/add | solution.py:38
  12.6 6.3 %all-to-all-start = ((f32[8,24,320]{2,1,0:T(8,128)}), f32[8,24,320]{2,1,0:T(8,128)S(1)}, u32[]{:S(2)}, u32[]{:S(2)}) async-start(f32[8,24,320]{2,1,0:T(8,128)} %dynamic-slice_add_fusion), calls=%async_computation | async-start | bytes 589824 | tf_op jit(solution)/shard_map/all_to_all | solution.py:41
  18.9 0.0 all-reduce.2.cloned.1.call-start
  18.9 9.6 %all-to-all-done = f32[8,24,320]{2,1,0:T(8,128)S(1)} async-done(((f32[8,24,320]{2,1,0:T(8,128)}), f32[8,24,320]{2,1,0:T(8,128)S(1)}, u32[]{:S(2)}, u32[]{:S(2)}) %all-to-all-start) | async-done | bytes 245792 | tf_op jit(solution)/shard_map/all_to_all | solution.py:41
  28.5 1.1 %fusion.14 = f32[2,96,96]{2,1,0:T(8,128)} fusion(f32[2,96,320]{2,1,0:T(8,128)S(1)} %bitcast.43), kind=kOutput, calls=%fused_computation.31 | convolution fusion | flops 70778880 | bytes 319488 | tf_op jit(solution)/shard_map/kij,klj->kil/dot_general | solution.py:42
  29.7 0.0 all-reduce.2.cloned.1.call-update
  29.7 50.6 %all-reduce.2.cloned.1.call-done = f32[2,96,96]{2,1,0:T(8,128)} async-done(((f32[2,96,96]{2,1,0:T(8,128)}), f32[2,96,96]{2,1,0:T(8,128)}) %all-reduce.2.cloned.1.call-update) | async-done | bytes 73744 | tf_op jit(solution)/shard_map/psum | solution.py:43
  80.3 1.0 select_reduce_fusion
  81.3 1.4 %fusion = f32[2,96,96]{2,1,0:T(8,128)S(1)} fusion(f32[2,96,96]{2,1,0:T(8,128)} %all-reduce.2.cloned.1.call-done, f32[2]{0:T(128)S(1)} %get-tuple-element.3, f32[96,96]{1,0:T(8,128)S(1)} %broadcast_select_fusion, pred[2]{0:T(512)(128)(4,1)S(1)} %broadcast_compare_fusion), kind=kOutput, calls=%fused_computation.8 | convolution fusion | flops 21417984 | bytes 184330 | tf_op jit(solution)/shard_map/kij,kjl->kil/dot_general | solution.py:14
  82.7 1.2 %fusion.5 = f32[2,96,96]{2,1,0:T(8,128)S(1)} fusion(f32[2,96,96]{2,1,0:T(8,128)S(1)} %fusion, f32[2,96,96]{2,1,0:T(8,128)} %all-reduce.2.cloned.1.call-done, f32[2]{0:T(128)S(1)} %get-tuple-element.3, pred[2]{0:T(512)(128)(4,1)S(1)} %broadcast_compare_fusion), kind=kOutput, calls=%fused_computation.17 | convolution fusion | flops 21288960 | bytes 221194 | tf_op jit(solution)/shard_map/kij,kjl->kil/dot_general | solution.py:14
  83.9 0.2 fusion.15
  84.1 0.2 fusion.1
  84.4 0.0 copy-done.1
  84.4 0.2 fusion.22
  84.6 0.2 fusion.16
  84.9 0.2 fusion.17
  85.1 0.2 fusion.2
  85.4 0.2 fusion.18
  85.6 0.2 fusion.23
  85.8 0.2 fusion.19
  86.1 0.2 fusion.3
  86.3 0.2 fusion.20
  86.5 0.2 fusion.24
  86.8 0.2 fusion.21
  87.0 0.2 fusion.4
  87.3 0.2 convolution_multiply_fusion
  87.5 0.4 convolution_convert_fusion
  87.9 0.1 copy.7
  88.0 11.5 %all_to_all.36 = bf16[2,96,320]{2,0,1:T(2,128)(2,1)S(1)} all-to-all(bf16[2,96,320]{2,0,1:T(2,128)(2,1)S(1)} %copy.7), channel_id=1, replica_groups=mesh['rep'=8,'shard'=4] {'shard'}, dimensions={1} | all-to-all | bytes 245760 | tf_op jit(solution)/shard_map/all_to_all | solution.py:45
  99.5 0.7 copy.8
  (5 shorter events, 0.1 us)
Async XLA Ops:
  7.2 2.9 %copy-start = (bf16[8,24,2560]{2,1,0:T(8,128)(2,1)S(1)}, bf16[8,24,2560]{2,1,0:T(8,128)(2,1)}, u32[]{:S(2)}) copy-start(bf16[8,24,2560]{2,1,0:T(8,128)(2,1)} %param.2) | copy-start | bytes 2949124
  7.2 2.9 %copy-start.2 = (f32[8,24,2560]{2,1,0:T(8,128)S(1)}, f32[8,24,2560]{2,1,0:T(8,128)}, u32[]{:S(2)}) copy-start(f32[8,24,2560]{2,1,0:T(8,128)} %param.3) | copy-start | bytes 5898244
  10.3 74.1 %copy-start.1 = (f32[8,24,2560]{2,1,0:T(8,128)}, f32[8,24,2560]{2,1,0:T(8,128)S(1)}, u32[]{:S(2)}) copy-start(f32[8,24,2560]{2,1,0:T(8,128)S(1)} %multiply_add_fusion) | copy-start | bytes 5898244
  12.6 15.9 %all-to-all-start = ((f32[8,24,320]{2,1,0:T(8,128)}), f32[8,24,320]{2,1,0:T(8,128)S(1)}, u32[]{:S(2)}, u32[]{:S(2)}) async-start(f32[8,24,320]{2,1,0:T(8,128)} %dynamic-slice_add_fusion), calls=%async_computation | async-start | bytes 589824 | tf_op jit(solution)/shard_map/all_to_all | solution.py:41
  18.9 61.4 %all-reduce.2.cloned.1.call-start = ((), (), s32[]{:S(2)}) async-start(), calls=%async_computation.2 | async-start | bytes 196608 | tf_op jit(solution)/shard_map/psum | solution.py:43
Sparse Core Ops, SparseCore 0:
  29.8 50.4 all-reduce.1
where the time goes:
time: 107 us
  waiting for transfers between devices  60.2 us (56%)
  between operations  14.2 us (13%)
  blocking collectives  11.5 us (11%)
  matrix products  7.54 us (7%)
  other arithmetic  6.41 us (6%)
  starting transfers between devices  6.32 us (6%)
    psum x1, waiting for transfers between devices, per_device_plain(): factor = schulz_factor(lax.psum(gram, 'rep'), scale)  50.6 us
    all_to_all x1, blocking collectives, per_device_plain(): lax.all_to_all(out, 'shard', split_axis=1, concat_axis=0, tiled=True)  11.5 us
    all_to_all x1, waiting for transfers between devices, per_device_plain(): lax.all_to_all(mine, 'shard', split_axis=0, concat_axis=1, tiled=True)  9.6 us
    dot_general x18, matrix products, mm(): return jnp.einsum('kij,kjl->kil', a, b, precision=lax.Precision.HIGHEST)  6.43 us
    all_to_all x1, starting transfers between devices, per_device_plain(): lax.all_to_all(mine, 'shard', split_axis=0, concat_axis=1, tiled=True)  6.32 us
    convert_element_type x1, other arithmetic, per_device_plain(): grads = gradients.astype(jnp.float32)  2.87 us
    add x1, other arithmetic, per_device_plain(): effective = grads + momentum_decay * new_momentum  2.25 us
  transfers between devices with their start and end apart: 2, of which 2 were waited for; matrix products, arithmetic and copies ran while one was open for 0% of the time, Pallas kernels for 0%

commit v1 on v0

--- a/solution.py
+++ b/solution.py
@@ -40,7 +40,7 @@
     mine = lax.dynamic_slice_in_dim(effective, lax.axis_index("rep") * cols, cols, 2)
     whole = lax.all_to_all(mine, "shard", split_axis=0, concat_axis=1, tiled=True)
     gram = jnp.einsum("kij,klj->kil", whole, whole, precision=lax.Precision.HIGHEST)
-    factor = schulz_factor(lax.psum(gram, "rep"), scale)
+    factor = schulz_factor(jnp.sum(lax.all_gather(gram, "rep"), axis=0), scale)
     out = mm(factor, whole).astype(jnp.bfloat16)
     return (lax.all_to_all(out, "shard", split_axis=1, concat_axis=0, tiled=True), new_momentum)
 

time: 107 us -> 48.4 us (0.45)
  waiting for transfers between devices: 60.2 us -> 9.59 us
  between operations: 14.2 us -> 0.85 us
  blocking collectives: 11.5 us -> 20 us
  matrix products: 7.54 us -> 4.94 us
    psum x1 -> x0, waiting for transfers between devices: 50.6 us -> none  [per_device_plain(): factor = schulz_factor(lax.psum(gram, 'rep'), scale)]
    all_gather x0 -> x1, blocking collectives: none -> 10.4 us  [per_device_plain(): factor = schulz_factor(jnp.sum(lax.all_gather(gram, 'rep'), axis=0), scale)]
    dot_general x18, matrix products: 6.43 us -> 4.48 us  [mm(): return jnp.einsum('kij,kjl->kil', a, b, precision=lax.Precision.HIGHEST)]
    all_to_all x1, blocking collectives: 11.5 us -> 9.6 us  [per_device_plain(): lax.all_to_all(out, 'shard', split_axis=1, concat_axis=0, tiled=True)]
  transfers between devices with their start and end apart: 2 -> 1, of which waited for: 2 -> 1; matrix products, arithmetic and copies ran while one was open for 0% -> 0% of each run, Pallas kernels for 0% -> 0%
where the time goes in v1:
time: 48.4 us; the launch traced here: 48.1 us
  blocking collectives  20 us (41%)
  waiting for transfers between devices  9.59 us (20%)
  starting transfers between devices  6.32 us (13%)
  other arithmetic  5.56 us (11%)
  matrix products  4.94 us (10%)
  between operations  0.85 us (2%)
  local copies, waits for them, and re-layouts  0.83 us (2%)
    all_gather x1, blocking collectives, per_device_plain(): factor = schulz_factor(jnp.sum(lax.all_gather(gram, 'rep'), axis=0), scale)  10.4 us
    all_to_all x1, blocking collectives, per_device_plain(): lax.all_to_all(out, 'shard', split_axis=1, concat_axis=0, tiled=True)  9.6 us
    all_to_all x1, waiting for transfers between devices, per_device_plain(): lax.all_to_all(mine, 'shard', split_axis=0, concat_axis=1, tiled=True)  9.59 us
    all_to_all x1, starting transfers between devices, per_device_plain(): lax.all_to_all(mine, 'shard', split_axis=0, concat_axis=1, tiled=True)  6.32 us
    dot_general x18, matrix products, mm(): return jnp.einsum('kij,kjl->kil', a, b, precision=lax.Precision.HIGHEST)  4.48 us
    convert_element_type x1, other arithmetic, per_device_plain(): grads = gradients.astype(jnp.float32)  2.85 us
    add x1, other arithmetic, per_device_plain(): effective = grads + momentum_decay * new_momentum  2.24 us
  transfers between devices with their start and end apart: 1, of which 1 were waited for; matrix products, arithmetic and copies ran while one was open for 0% of the time, Pallas kernels for 0%

profile of v1, /device:TPU:0, one launch (start us, length us, event | category | flops | bytes accessed | tf_op | source)
XLA Modules:
  0.0 48.1 jit_solution(4712804642404557580)
XLA Ops:
  0.6 0.0 copy-start
  0.6 0.0 copy-start.2
  0.7 2.9 %convert_element_type.7 = f32[8,24,2560]{2,1,0:T(8,128)} convert(bf16[8,24,2560]{2,1,0:T(8,128)(2,1)} %param.2) | non-fusion elementwise | flops 491520 | bytes 2949120 | tf_op jit(solution)/shard_map/convert_element_type | solution.py:36
  3.5 0.0 copy-done
  3.5 0.0 copy-done.2
  3.5 0.3 multiply_add_fusion
  3.8 0.0 copy-start.1
  3.8 2.2 %dynamic-slice_add_fusion = f32[8,24,320]{2,1,0:T(8,128)} fusion(f32[8,24,2560]{2,1,0:T(8,128)} %convert_element_type.7, s32[]{:T(128)S(6)} %select_n.12, f32[8,24,2560]{2,1,0:T(8,128)S(1)} %multiply_add_fusion), kind=kLoop, calls=%fused_computation.13 | loop fusion | flops 122880 | bytes 737284 | tf_op jit(solution)/shard_map/add | solution.py:38
  6.0 6.3 %all-to-all-start = ((f32[8,24,320]{2,1,0:T(8,128)}), f32[8,24,320]{2,1,0:T(8,128)S(1)}, u32[]{:S(2)}, u32[]{:S(2)}) async-start(f32[8,24,320]{2,1,0:T(8,128)} %dynamic-slice_add_fusion), calls=%async_computation | async-start | bytes 589824 | tf_op jit(solution)/shard_map/all_to_all | solution.py:41
  12.4 9.6 %all-to-all-done = f32[8,24,320]{2,1,0:T(8,128)S(1)} async-done(((f32[8,24,320]{2,1,0:T(8,128)}), f32[8,24,320]{2,1,0:T(8,128)S(1)}, u32[]{:S(2)}, u32[]{:S(2)}) %all-to-all-start) | async-done | bytes 245792 | tf_op jit(solution)/shard_map/all_to_all | solution.py:41
  22.0 0.5 fusion.14
  22.5 10.4 %all-gather = f32[16,96,96]{2,1,0:T(8,128)S(1)} all-gather(f32[2,96,96]{2,1,0:T(8,128)S(1)} %fusion.14), channel_id=2, replica_groups=mesh['rep'=8,'shard'=4] {'rep'}, dimensions={0}, use_global_device_ids=true | all-gather | bytes 663552 | tf_op jit(solution)/shard_map/all_gather | solution.py:43
  32.9 0.1 reduce_sum.19
  32.9 0.0 copy-done.1
  32.9 0.1 select_reduce_fusion
  33.1 0.3 fusion
  33.4 0.3 fusion.5
  33.7 0.2 fusion.15
  34.0 0.2 fusion.1
  34.2 0.2 fusion.22
  34.4 0.2 fusion.16
  34.7 0.2 fusion.17
  34.9 0.2 fusion.2
  35.2 0.2 fusion.18
  35.4 0.2 fusion.23
  35.6 0.2 fusion.19
  35.9 0.2 fusion.3
  36.1 0.2 fusion.20
  36.4 0.2 fusion.24
  36.6 0.2 fusion.21
  36.8 0.2 fusion.4
  37.1 0.2 convolution_multiply_fusion
  37.3 0.4 convolution_convert_fusion
  37.7 0.1 copy.7
  37.8 9.6 %all_to_all.36 = bf16[2,96,320]{2,0,1:T(2,128)(2,1)S(1)} all-to-all(bf16[2,96,320]{2,0,1:T(2,128)(2,1)S(1)} %copy.7), channel_id=1, replica_groups=mesh['rep'=8,'shard'=4] {'shard'}, dimensions={1} | all-to-all | bytes 245760 | tf_op jit(solution)/shard_map/all_to_all | solution.py:45
  47.4 0.7 %copy.8 = bf16[4,2,24,320]{3,2,1,0:T(8,128)(2,1)} copy(bf16[4,2,24,320]{3,1,2,0:T(2,128)(2,1)S(1)} %bitcast.48) | data formatting | bytes 245760 | tf_op jit(solution)/shard_map/all_to_all | solution.py:45
  (5 shorter events, 0.1 us)
Async XLA Ops:
  0.6 2.9 %copy-start = (bf16[8,24,2560]{2,1,0:T(8,128)(2,1)S(1)}, bf16[8,24,2560]{2,1,0:T(8,128)(2,1)}, u32[]{:S(2)}) copy-start(bf16[8,24,2560]{2,1,0:T(8,128)(2,1)} %param.2) | copy-start | bytes 2949124
  0.6 2.9 %copy-start.2 = (f32[8,24,2560]{2,1,0:T(8,128)S(1)}, f32[8,24,2560]{2,1,0:T(8,128)}, u32[]{:S(2)}) copy-start(f32[8,24,2560]{2,1,0:T(8,128)} %param.3) | copy-start | bytes 5898244
  3.8 29.2 %copy-start.1 = (f32[8,24,2560]{2,1,0:T(8,128)}, f32[8,24,2560]{2,1,0:T(8,128)S(1)}, u32[]{:S(2)}) copy-start(f32[8,24,2560]{2,1,0:T(8,128)S(1)} %multiply_add_fusion) | copy-start | bytes 5898244
  6.0 15.9 %all-to-all-start = ((f32[8,24,320]{2,1,0:T(8,128)}), f32[8,24,320]{2,1,0:T(8,128)S(1)}, u32[]{:S(2)}, u32[]{:S(2)}) async-start(f32[8,24,320]{2,1,0:T(8,128)} %dynamic-slice_add_fusion), calls=%async_computation | async-start | bytes 589824 | tf_op jit(solution)/shard_map/all_to_all | solution.py:41

commit v2 on v0

--- a/solution.py
+++ b/solution.py
@@ -38,7 +38,10 @@
     effective = grads + momentum_decay * new_momentum
     cols = width // replicas
     mine = lax.dynamic_slice_in_dim(effective, lax.axis_index("rep") * cols, cols, 2)
-    whole = lax.all_to_all(mine, "shard", split_axis=0, concat_axis=1, tiled=True)
+    whole = jnp.concatenate(
+        lax.all_to_all(jnp.stack(jnp.split(mine, lax.axis_size("shard"), axis=0)), "shard", 0, 0),
+        axis=1,
+    )
     gram = jnp.einsum("kij,klj->kil", whole, whole, precision=lax.Precision.HIGHEST)
     factor = schulz_factor(lax.psum(gram, "rep"), scale)
     out = mm(factor, whole).astype(jnp.bfloat16)

time: 107 us -> 107 us (level)
  no operation moved by 1% of the time
where the time goes in v2:
time: 107 us
  waiting for transfers between devices  60.2 us (56%)
  between operations  14.2 us (13%)
  blocking collectives  11.5 us (11%)
  matrix products  7.54 us (7%)
  other arithmetic  6.43 us (6%)
  starting transfers between devices  6.32 us (6%)
    psum x1, waiting for transfers between devices, per_device_plain(): factor = schulz_factor(lax.psum(gram, 'rep'), scale)  50.6 us
    all_to_all x1, blocking collectives, per_device_plain(): lax.all_to_all(out, 'shard', split_axis=1, concat_axis=0, tiled=True)  11.5 us
    all_to_all x1, waiting for transfers between devices, per_device_plain(): lax.all_to_all(jnp.stack(jnp.split(mine, lax.axis_size('shard'), axis=0))...  9.6 us
    dot_general x18, matrix products, mm(): return jnp.einsum('kij,kjl->kil', a, b, precision=lax.Precision.HIGHEST)  6.43 us
    all_to_all x1, starting transfers between devices, per_device_plain(): lax.all_to_all(jnp.stack(jnp.split(mine, lax.axis_size('shard'), axis=0))...  6.32 us
    convert_element_type x1, other arithmetic, per_device_plain(): grads = gradients.astype(jnp.float32)  2.86 us
  transfers between devices with their start and end apart: 2, of which 2 were waited for; matrix products, arithmetic and copies ran while one was open for 0% of the time, Pallas kernels for 0%

profile of v2, /device:TPU:0, one launch (start us, length us, event | category | flops | bytes accessed | tf_op | source)
XLA Modules:
  0.0 107.0 jit_solution(12393420851496176867)
XLA Ops:
  7.2 0.0 copy-start
  7.2 0.0 copy-start.2
  7.2 2.9 %convert_element_type.7 = f32[8,24,2560]{2,1,0:T(8,128)} convert(bf16[8,24,2560]{2,1,0:T(8,128)(2,1)} %param.2) | non-fusion elementwise | flops 491520 | bytes 2949120 | tf_op jit(solution)/shard_map/convert_element_type | solution.py:36
  10.1 0.0 copy-done
  10.1 0.0 copy-done.2
  10.1 0.3 multiply_add_fusion
  10.3 0.0 copy-start.1
  10.3 1.5 %dynamic-slice_add_fusion = f32[8,24,320]{2,1,0:T(8,128)S(1)} fusion(f32[8,24,2560]{2,1,0:T(8,128)} %convert_element_type.7, s32[]{:T(128)S(6)} %select_n.12, f32[8,24,2560]{2,1,0:T(8,128)S(1)} %multiply_add_fusion), kind=kLoop, calls=%fused_computation.13 | loop fusion | flops 122880 | bytes 737284 | tf_op jit(solution)/shard_map/add | solution.py:38
  11.9 0.7 pad_maximum_fusion
  12.6 6.3 %all-to-all-start = ((f32[4,2,24,320]{3,2,1,0:T(8,128)}), f32[4,2,24,320]{3,2,1,0:T(8,128)S(1)}, u32[]{:S(2)}, u32[]{:S(2)}) async-start(f32[4,2,24,320]{3,2,1,0:T(8,128)} %pad_maximum_fusion), calls=%async_computation | async-start | bytes 589824 | tf_op jit(solution)/shard_map/all_to_all | solution.py:42
  19.0 0.0 all-reduce.2.cloned.1.call-start
  19.0 9.6 %all-to-all-done = f32[4,2,24,320]{3,2,1,0:T(8,128)S(1)} async-done(((f32[4,2,24,320]{3,2,1,0:T(8,128)}), f32[4,2,24,320]{3,2,1,0:T(8,128)S(1)}, u32[]{:S(2)}, u32[]{:S(2)}) %all-to-all-start) | async-done | bytes 245792 | tf_op jit(solution)/shard_map/all_to_all | solution.py:42
  28.6 1.1 %fusion.14 = f32[2,96,96]{2,1,0:T(8,128)} fusion(f32[2,96,320]{2,1,0:T(8,128)S(1)} %bitcast.49), kind=kOutput, calls=%fused_computation.36 | convolution fusion | flops 70778880 | bytes 319488 | tf_op jit(solution)/shard_map/kij,klj->kil/dot_general | solution.py:45
  29.7 0.0 copy-done.1
  29.7 0.0 all-reduce.2.cloned.1.call-update
  29.8 50.6 %all-reduce.2.cloned.1.call-done = f32[2,96,96]{2,1,0:T(8,128)} async-done(((f32[2,96,96]{2,1,0:T(8,128)}), f32[2,96,96]{2,1,0:T(8,128)}) %all-reduce.2.cloned.1.call-update) | async-done | bytes 73744 | tf_op jit(solution)/shard_map/psum | solution.py:46
  80.3 1.0 select_reduce_fusion
  81.4 1.4 %fusion = f32[2,96,96]{2,1,0:T(8,128)S(1)} fusion(f32[2,96,96]{2,1,0:T(8,128)} %all-reduce.2.cloned.1.call-done, f32[2]{0:T(128)S(1)} %get-tuple-element.3, f32[96,96]{1,0:T(8,128)S(1)} %broadcast_select_fusion, pred[2]{0:T(512)(128)(4,1)S(1)} %broadcast_compare_fusion), kind=kOutput, calls=%fused_computation.8 | convolution fusion | flops 21417984 | bytes 184330 | tf_op jit(solution)/shard_map/kij,kjl->kil/dot_general | solution.py:14
  82.8 1.2 %fusion.5 = f32[2,96,96]{2,1,0:T(8,128)S(1)} fusion(f32[2,96,96]{2,1,0:T(8,128)S(1)} %fusion, f32[2,96,96]{2,1,0:T(8,128)} %all-reduce.2.cloned.1.call-done, f32[2]{0:T(128)S(1)} %get-tuple-element.3, pred[2]{0:T(512)(128)(4,1)S(1)} %broadcast_compare_fusion), kind=kOutput, calls=%fused_computation.18 | convolution fusion | flops 21288960 | bytes 221194 | tf_op jit(solution)/shard_map/kij,kjl->kil/dot_general | solution.py:14
  84.0 0.2 fusion.15
  84.2 0.2 fusion.1
  84.4 0.2 fusion.22
  84.7 0.2 fusion.16
  84.9 0.2 fusion.17
  85.2 0.2 fusion.2
  85.4 0.2 fusion.18
  85.6 0.2 fusion.23
  85.9 0.2 fusion.19
  86.1 0.2 fusion.3
  86.3 0.2 fusion.20
  86.6 0.2 fusion.24
  86.8 0.2 fusion.21
  87.1 0.2 fusion.4
  87.3 0.2 convolution_multiply_fusion
  87.5 0.4 convolution_convert_fusion
  87.9 0.1 copy.7
  88.1 11.5 %all_to_all.23 = bf16[2,96,320]{2,0,1:T(2,128)(2,1)S(1)} all-to-all(bf16[2,96,320]{2,0,1:T(2,128)(2,1)S(1)} %copy.7), channel_id=1, replica_groups=mesh['rep'=8,'shard'=4] {'shard'}, dimensions={1} | all-to-all | bytes 245760 | tf_op jit(solution)/shard_map/all_to_all | solution.py:48
  99.5 0.7 copy.8
  (6 shorter events, 0.1 us)
Async XLA Ops:
  7.2 2.9 %copy-start = (bf16[8,24,2560]{2,1,0:T(8,128)(2,1)S(1)}, bf16[8,24,2560]{2,1,0:T(8,128)(2,1)}, u32[]{:S(2)}) copy-start(bf16[8,24,2560]{2,1,0:T(8,128)(2,1)} %param.2) | copy-start | bytes 2949124
  7.2 2.9 %copy-start.2 = (f32[8,24,2560]{2,1,0:T(8,128)S(1)}, f32[8,24,2560]{2,1,0:T(8,128)}, u32[]{:S(2)}) copy-start(f32[8,24,2560]{2,1,0:T(8,128)} %param.3) | copy-start | bytes 5898244
  10.3 19.4 %copy-start.1 = (f32[8,24,2560]{2,1,0:T(8,128)}, f32[8,24,2560]{2,1,0:T(8,128)S(1)}, u32[]{:S(2)}) copy-start(f32[8,24,2560]{2,1,0:T(8,128)S(1)} %multiply_add_fusion) | copy-start | bytes 5898244
  12.6 15.9 %all-to-all-start = ((f32[4,2,24,320]{3,2,1,0:T(8,128)}), f32[4,2,24,320]{3,2,1,0:T(8,128)S(1)}, u32[]{:S(2)}, u32[]{:S(2)}) async-start(f32[4,2,24,320]{3,2,1,0:T(8,128)} %pad_maximum_fusion), calls=%async_computation | async-start | bytes 589824 | tf_op jit(solution)/shard_map/all_to_all | solution.py:42
  19.0 61.4 %all-reduce.2.cloned.1.call-start = ((), (), s32[]{:S(2)}) async-start(), calls=%async_computation.2 | async-start | bytes 196608 | tf_op jit(solution)/shard_map/psum | solution.py:46
Sparse Core Ops, SparseCore 0:
  29.9 50.4 all-reduce.1
